TPU v7x, 256 devices: a whole 4x4x8 slice. The times are simulated.
256 devices in a mesh: row: 8 (over y, x_hi), col: 8 (over z), depth: 4 (over x_lo, core).
Axes of the slice: x: 4 (x_hi: 2, x_lo: 2; x = x_hi * 2 + x_lo), y: 4, z: 8, core: 2. Of those that a mesh axis runs over, the one named last changes fastest.
Arguments:
- inputs: bfloat16 [1024, 7168], P(('depth', 'col'), 'row'), may hold values from -6 to 6
- out_grad: bfloat16 [1024, 7168], P(('depth', 'col'), 'row'), may hold values from -6 to 6
- w_gate: bfloat16 [7168, 15360], P('row', 'col'), may hold values from -0.0625 to 0.0625
- w_up: bfloat16 [7168, 15360], P('row', 'col'), may hold values from -0.0625 to 0.0625
- w_down: bfloat16 [15360, 7168], P('col', 'row'), may hold values from -0.046875 to 0.046875
Outputs:
- input_grad: bfloat16 [1024, 7168], P(('depth', 'col'), 'row')
- gate_grad: bfloat16 [7168, 15360], P(('row', 'depth'), 'col')
- up_grad: bfloat16 [7168, 15360], P(('row', 'depth'), 'col')
- down_grad: bfloat16 [15360, 7168], P(('col', 'depth'), 'row')
All inputs are finite; a program needn't handle non-finite values.
Results may differ from a plain program's by a relative error of at most 0.005.
Values may be sent and summed in bfloat16 or wider, within the bound.
A program may use at most 128 MiB of HBM per device.

v0:
```python
import jax
import jax.numpy as jnp
from jax import lax
from jax.sharding import PartitionSpec as P


def contract_last(left, right):
    return lax.dot_general(
        left, right, (((1,), (1,)), ((), ())), preferred_element_type=jnp.float32
    )


def contract_first(left, right):
    return lax.dot_general(
        left, right, (((0,), (0,)), ((), ())), preferred_element_type=jnp.float32
    )


def on_device(inputs, out_grad, w_gate, w_up, w_down):
    token_rows, grad_rows = (
        lax.all_gather(inputs, "col", axis=0, tiled=True),
        lax.all_gather(out_grad, "col", axis=0, tiled=True),
    )
    hidden_width = w_gate.shape[1]
    gate_part = jnp.dot(token_rows, w_gate, preferred_element_type=jnp.float32)
    up_part = jnp.dot(token_rows, w_up, preferred_element_type=jnp.float32)
    back_part = contract_last(grad_rows, w_down)
    summed = lax.psum_scatter(
        jnp.concatenate([gate_part, up_part, back_part], axis=1),
        "row",
        scatter_dimension=0,
        tiled=True,
    )
    gate_val = summed[:, :hidden_width]
    up_val = summed[:, hidden_width : 2 * hidden_width]
    hidden_grad = summed[:, 2 * hidden_width :]
    sigma = jax.nn.sigmoid(gate_val)
    hidden = (gate_val * sigma * up_val).astype(jnp.bfloat16)
    gate_back = (hidden_grad * up_val * sigma * (1.0 + gate_val * (1.0 - sigma))).astype(
        jnp.bfloat16
    )
    up_back = (hidden_grad * gate_val * sigma).astype(jnp.bfloat16)
    gate_rows, up_rows, hidden_rows = (
        lax.all_gather(gate_back, "row", axis=0, tiled=True),
        lax.all_gather(up_back, "row", axis=0, tiled=True),
        lax.all_gather(hidden, "row", axis=0, tiled=True),
    )
    input_grad = lax.psum_scatter(
        contract_last(gate_rows, w_gate) + contract_last(up_rows, w_up),
        "col",
        scatter_dimension=0,
        tiled=True,
    ).astype(jnp.bfloat16)
    gate_part = contract_first(token_rows, gate_rows)
    up_part = contract_first(token_rows, up_rows)
    down_part = contract_first(hidden_rows, grad_rows)
    gate_grad, up_grad, down_grad = (
        lax.psum_scatter(gate_part, "depth", scatter_dimension=0, tiled=True),
        lax.psum_scatter(up_part, "depth", scatter_dimension=0, tiled=True),
        lax.psum_scatter(down_part, "depth", scatter_dimension=0, tiled=True),
    )
    return (
        input_grad,
        gate_grad.astype(jnp.bfloat16),
        up_grad.astype(jnp.bfloat16),
        down_grad.astype(jnp.bfloat16),
    )


def solution(mesh):
    placed = (
        P(("depth", "col"), "row"),
        P(("depth", "col"), "row"),
        P("row", "col"),
        P("row", "col"),
        P("col", "row"),
    )
    return jax.shard_map(
        on_device,
        mesh=mesh,
        in_specs=placed,
        out_specs=(
            P(("depth", "col"), "row"),
            P(("row", "depth"), "col"),
            P(("row", "depth"), "col"),
            P(("col", "depth"), "row"),
        ),
        check_vma=False,
    )
```

profile of v0, /device:TPU:1, one launch (start us, length us, event | category | flops | bytes accessed | tf_op | source)
XLA Modules:
  0.0 518.1 jit_solution(7887453463775163824)
XLA Ops:
  7.2 0.0 copy-start
  7.2 0.0 reduce-scatter.10.cloned.1.call-start
  7.2 0.0 copy-start.9
  7.2 24.0 %all_gather.15 = bf16[256,896]{1,0:T(8,128)(2,1)S(1)} all-gather(bf16[32,896]{1,0:T(8,128)(2,1)} %param.5), channel_id=1, replica_groups=mesh['row'=8,'col'=8,'depth'=4] {'col'}, dimensions={0}, use_global_device_ids=true | all-gather | bytes 516096 | tf_op jit(solution)/shard_map/all_gather | solution.py:21
  31.2 0.0 copy-done
  31.2 0.0 copy-start.2
  31.2 1.2 fusion
  32.5 0.0 copy-done.9
  32.5 0.0 copy-start.12
  32.5 0.0 copy-start.8
  32.5 1.2 fusion.1
  33.8 0.0 copy-done.2
  33.8 0.0 copy-done.12
  33.8 18.9 %all_gather.16 = bf16[256,896]{1,0:T(8,128)(2,1)S(1)} all-gather(bf16[32,896]{1,0:T(8,128)(2,1)S(1)} %copy-done.12), channel_id=1, replica_groups=mesh['row'=8,'col'=8,'depth'=4] {'col'}, dimensions={0}, use_global_device_ids=true | all-gather | bytes 516096 | tf_op jit(solution)/shard_map/all_gather | solution.py:22
  52.7 0.0 copy-start.6
  52.7 0.8 copy-done.6
  53.4 0.0 copy-done.8
  53.4 1.3 fusion.2
  54.7 2.9 pad_maximum_fusion
  57.6 0.0 reduce-scatter.10.cloned.1.call-update
  57.7 0.0 reduce-scatter.12.cloned.1.call-start
  57.7 111.4 %reduce-scatter.10.cloned.1.call-done = f32[32,5760]{1,0:T(8,128)} async-done(((f32[256,5760]{1,0:T(8,128)}), f32[32,5760]{1,0:T(8,128)}) %reduce-scatter.10.cloned.1.call-update) | async-done | bytes 737296 | tf_op jit(solution)/shard_map/reduce_scatter | solution.py:28
  169.2 2.0 multiply_convert_fusion
  171.1 32.9 %all_gather.17 = bf16[256,1920]{1,0:T(8,128)(2,1)S(1)} all-gather(bf16[32,1920]{1,0:T(8,128)(2,1)S(1)} %get-tuple-element.13), channel_id=1, replica_groups=mesh['row'=8,'col'=8,'depth'=4] {'row'}, dimensions={0}, use_global_device_ids=true | all-gather | bytes 1105920 | tf_op jit(solution)/shard_map/all_gather | solution.py:44
  204.0 0.0 copy-start.4
  204.0 0.0 copy-start.10
  204.0 1.3 fusion.3
  205.3 0.0 copy-done.4
  205.3 32.8 %all_gather.18 = bf16[256,1920]{1,0:T(8,128)(2,1)S(1)} all-gather(bf16[32,1920]{1,0:T(8,128)(2,1)S(1)} %get-tuple-element.14), channel_id=1, replica_groups=mesh['row'=8,'col'=8,'depth'=4] {'row'}, dimensions={0}, use_global_device_ids=true | all-gather | bytes 1105920 | tf_op jit(solution)/shard_map/all_gather | solution.py:45
  238.1 0.0 copy-done.10
  238.1 0.0 copy-start.3
  238.1 0.0 copy-start.5
  238.1 2.2 convolution_add_fusion
  240.4 0.0 reduce-scatter.12.cloned.1.call-update
  240.4 0.0 reduce-scatter.16.cloned.1.call-start
  240.4 0.0 copy-done.3
  240.4 0.0 copy-done.5
  240.5 4.1 convolution_bitcast_fusion.1
  244.5 8.5 %copy.13 = f32[896,1920]{1,0:T(8,128)} copy(f32[896,1920]{0,1:T(8,128)} %convolution_bitcast_fusion.1) | data formatting | bytes 13762560
  253.0 0.0 reduce-scatter.16.cloned.1.call-update
  253.0 0.0 reduce-scatter.18.cloned.1.call-start
  253.1 4.1 convolution_bitcast_fusion
  257.2 8.4 %copy.15 = f32[896,1920]{1,0:T(8,128)} copy(f32[896,1920]{0,1:T(8,128)} %convolution_bitcast_fusion) | data formatting | bytes 13762560
  265.6 0.0 copy-start.11
  265.6 0.0 copy-start.7
  265.6 0.0 reduce-scatter.18.cloned.1.call-update
  265.6 0.0 reduce-scatter.14.cloned.1.call-start
  265.7 0.8 copy-done.11
  266.5 32.2 %all_gather.19 = bf16[256,1920]{1,0:T(8,128)(2,1)S(1)} all-gather(bf16[32,1920]{1,0:T(8,128)(2,1)S(1)} %copy-done.11), channel_id=1, replica_groups=mesh['row'=8,'col'=8,'depth'=4] {'row'}, dimensions={0}, use_global_device_ids=true | all-gather | bytes 1105920 | tf_op jit(solution)/shard_map/all_gather | solution.py:46
  298.7 0.0 copy-done.7
  298.7 4.8 fusion.4
  303.5 0.0 reduce-scatter.14.cloned.1.call-update
  303.5 0.0 reduce-scatter.12.cloned.1.call-done
  303.5 1.5 convert_element_type.23
  305.1 58.1 %reduce-scatter.16.cloned.1.call-done = f32[224,1920]{1,0:T(8,128)} async-done(((f32[896,1920]{1,0:T(8,128)}), f32[224,1920]{1,0:T(8,128)}) %reduce-scatter.16.cloned.1.call-update) | async-done | bytes 1720336
  363.2 2.4 copy.14
  365.6 0.0 copy-start.1
  365.6 2.3 copy.11
  367.9 67.8 %reduce-scatter.18.cloned.1.call-done = f32[224,1920]{1,0:T(8,128)} async-done(((f32[896,1920]{1,0:T(8,128)}), f32[224,1920]{1,0:T(8,128)}) %reduce-scatter.18.cloned.1.call-update) | async-done | bytes 1720336
  435.7 2.4 copy.16
  438.1 2.2 copy.12
  440.3 68.9 %reduce-scatter.14.cloned.1.call-done = f32[480,896]{1,0:T(8,128)} async-done(((f32[1920,896]{1,0:T(8,128)}), f32[480,896]{1,0:T(8,128)}) %reduce-scatter.14.cloned.1.call-update) | async-done | bytes 1720336 | tf_op jit(solution)/shard_map/reduce_scatter | solution.py:60
  509.1 2.5 convert_element_type.27
  511.6 0.0 copy-done.1
Async XLA Ops:
  7.2 24.1 %copy-start = (bf16[896,1920]{1,0:T(8,128)(2,1)S(1)}, bf16[896,1920]{1,0:T(8,128)(2,1)}, u32[]{:S(2)}) copy-start(bf16[896,1920]{1,0:T(8,128)(2,1)} %param.7) | copy-start | bytes 10321924
  7.2 162.0 %reduce-scatter.10.cloned.1.call-start = ((), (), s32[]{:S(2)}) async-start(), calls=%async_computation.5 | async-start | bytes 6635520 | tf_op jit(solution)/shard_map/reduce_scatter | solution.py:28
  7.2 25.3 %copy-start.9 = (bf16[896,1920]{1,0:T(8,128)(2,1)S(1)}, bf16[896,1920]{1,0:T(8,128)(2,1)}, u32[]{:S(2)}) copy-start(bf16[896,1920]{1,0:T(8,128)(2,1)} %param.8) | copy-start | bytes 10321924
  31.2 2.5 copy-start.2
  32.5 1.3 copy-start.12
  32.5 20.9 %copy-start.8 = (bf16[1920,896]{1,0:T(8,128)(2,1)S(1)}, bf16[1920,896]{1,0:T(8,128)(2,1)}, u32[]{:S(2)}) copy-start(bf16[1920,896]{1,0:T(8,128)(2,1)} %param.9) | copy-start | bytes 10321924
  52.7 0.8 copy-start.6
  57.7 245.9 %reduce-scatter.12.cloned.1.call-start = ((), (), s32[]{:S(2)}) async-start(), calls=%async_computation.6 | async-start | bytes 1032192 | tf_op jit(solution)/shard_map/reduce_scatter | solution.py:48
  204.0 1.3 copy-start.4
  204.0 34.1 %copy-start.10 = (bf16[896,1920]{1,0:T(8,128)(2,1)S(1)}, bf16[896,1920]{1,0:T(8,128)(2,1)}, u32[]{:S(2)}) copy-start(bf16[896,1920]{1,0:T(8,128)(2,1)} %param.8) | copy-start | bytes 10321924
  238.1 2.3 copy-start.3
  238.1 2.3 copy-start.5
  240.4 122.8 %reduce-scatter.16.cloned.1.call-start = ((), (), s32[]{:S(2)}) async-start(), calls=%async_computation.8 | async-start | bytes 8601600
  253.0 182.7 %reduce-scatter.18.cloned.1.call-start = ((), (), s32[]{:S(2)}) async-start(), calls=%async_computation.9 | async-start | bytes 8601600
  265.6 0.9 copy-start.11
  265.6 33.1 %copy-start.7 = (bf16[256,896]{1,0:T(8,128)(2,1)S(1)}, bf16[256,896]{1,0:T(8,128)(2,1)}, u32[]{:S(2)}) copy-start(bf16[256,896]{1,0:T(8,128)(2,1)} %copy-done.6) | copy-start | bytes 1376260
  265.6 243.5 %reduce-scatter.14.cloned.1.call-start = ((), (), s32[]{:S(2)}) async-start(), calls=%async_computation.7 | async-start | bytes 8601600 | tf_op jit(solution)/shard_map/reduce_scatter | solution.py:60
  365.6 146.0 %copy-start.1 = (bf16[896,1920]{1,0:T(8,128)(2,1)S(1)}, bf16[896,1920]{1,0:T(8,128)(2,1)}, u32[]{:S(2)}) copy-start(bf16[896,1920]{1,0:T(8,128)(2,1)} %param.7) | copy-start | bytes 10321924
Sparse Core Ops, SparseCore 0:
  57.8 111.3 reduce-scatter.9
  240.5 43.3 reduce-scatter.11
  286.7 76.4 reduce-scatter.15
  365.6 70.0 reduce-scatter.17
  438.3 70.8 reduce-scatter.13
where the time goes:
time: 519 us; the launch traced here: 518 us
  waiting for transfers between devices  306 us (59%)
  blocking collectives  141 us (27%)
  local copies, waits for them, and re-layouts  27.9 us (5%)
  matrix products  20.2 us (4%)
  between operations  13.9 us (3%)
  other arithmetic  8.86 us (2%)
    unnamed x7, waiting for transfers between devices  126 us
    reduce_scatter x1, waiting for transfers between devices, on_device(): lax.psum_scatter(jnp.concatenate([gate_part, up_part, back_part], axis=1)...  111 us
    reduce_scatter x1, waiting for transfers between devices, on_device(): lax.psum_scatter(down_part, 'depth', scatter_dimension=0, tiled=True)  68.9 us
    all_gather x1, blocking collectives, on_device(): lax.all_gather(gate_back, 'row', axis=0, tiled=True)  32.9 us
    all_gather x1, blocking collectives, on_device(): lax.all_gather(up_back, 'row', axis=0, tiled=True)  32.8 us
    all_gather x1, blocking collectives, on_device(): lax.all_gather(hidden, 'row', axis=0, tiled=True)  32.2 us
    unnamed x32, local copies, waits for them, and re-layouts  27.9 us
    all_gather x1, blocking collectives, on_device(): lax.all_gather(inputs, 'col', axis=0, tiled=True)  24 us
  transfers between devices with their start and end apart: 5, of which 4 were waited for; matrix products, arithmetic and copies ran while one was open for 8% of the time, Pallas kernels for 0%

commit v1 on v0

v1 whole, which is shorter than its diff:
```python
import jax
import jax.numpy as jnp
from jax import lax
from jax.experimental import pallas as pl
from jax.experimental.pallas import tpu as pltpu
from jax.sharding import PartitionSpec as P

MESH = pl.DeviceIdType.MESH
F32, BF16 = jnp.float32, jnp.bfloat16

DELTA = (0, 1, -1, 2, -2, 3, -3, 4)
SLOT = {1: 1, -1: 2, 2: 3, -2: 4, 3: 5, -3: 6, 4: 7, -4: 7}
DEEP = 4
STEPS = 8
ROWS = 32
WIDE = 896
FULL = 1920
OWN = 480
PAD = 512
WIN = 640
PIECE = 224


def mm(a, b):
    return lax.dot_general(a, b, (((1,), (0,)), ((), ())), preferred_element_type=F32)


def mm_t(a, b):
    return lax.dot_general(a, b, (((1,), (1,)), ((), ())), preferred_element_type=F32)


def kernel(
    x_hbm, dy_hbm, wg_hbm, wu_hbm, wd_hbm,
    ig_out, gu_out, down_out,
    xd, xt, win, w2, wd, part, part_own, psend, precv, ysum, xrecv, g,
    piece_send, piece_recv, down, ig, ig_core, ig_xs, ig_xr, ig_zs, ig_zr, ig_fin,
    load_sem, z_s, z_r, cf_s, cf_r, xf_s, xf_r, cb_s, cb_r, y_s, y_r, h_s, h_r,
    ah_s, ah_r, ay_s, ay_r, af_s, af_r, p_s, p_r, ic_s, ic_r, ix_s, ix_r, iz_s, iz_r, out_sem,
):
    row, z, dep = lax.axis_index("row"), lax.axis_index("col"), lax.axis_index("depth")
    y, xh = row // 2, row % 2
    xl, c = dep // 2, dep % 2
    dep_x = (1 - xl) * 2 + c
    dep_c = xl * 2 + 1 - c
    dep_xc = (1 - xl) * 2 + 1 - c

    def at_row(yy, hh):
        return {"row": yy * 2 + hh, "col": z, "depth": dep}

    def at_depth(d):
        return {"row": row, "col": z, "depth": d}

    def at_col(zz):
        return {"row": row, "col": zz, "depth": dep}

    def y_at(j):
        return at_row((y + j) % 4, xh)

    def remote(src, dst, ss, rs, dev):
        return pltpu.make_async_remote_copy(
            src_ref=src, dst_ref=dst, send_sem=ss, recv_sem=rs, device_id=dev, device_id_type=MESH
        )

    start = jnp.where(dep == 3, 1280, dep * 480 - (dep * 480) % 128)
    start = pl.multiple_of(start, 128)
    shift = dep * 480 - start
    loads = [
        pltpu.make_async_copy(x_hbm, xd.at[0, 0, dep], load_sem.at[0]),
        pltpu.make_async_copy(dy_hbm, xd.at[1, 0, dep], load_sem.at[1]),
        pltpu.make_async_copy(wg_hbm.at[:, pl.ds(start, WIN)], win.at[0], load_sem.at[2]),
        pltpu.make_async_copy(wu_hbm.at[:, pl.ds(start, WIN)], win.at[1], load_sem.at[3]),
        pltpu.make_async_copy(wd_hbm.at[pl.ds(dep * OWN, OWN)], wd.at[pl.ds(0, OWN)], load_sem.at[4]),
    ]
    for cp in loads:
        cp.start()

    barrier = pltpu.get_barrier_semaphore()
    peers = [at_depth(dep_x), at_depth(dep_c), at_depth(dep_xc)]
    peers += [at_col((z + m) % STEPS) for m in range(1, STEPS)]
    peers += [y_at(j) for j in (1, 2, 3)] + [at_row(y, 1 - xh)]
    for dev in peers:
        pl.semaphore_signal(barrier, inc=1, device_id=dev, device_id_type=MESH)
    pl.semaphore_wait(barrier, len(peers))

    loads[0].wait()
    loads[1].wait()

    def block(s, d):
        return xd.at[:, s, d]

    z_sends = []
    for m in (1, -1, 2, -2, 3, -3, 4):
        slot = SLOT[-m]
        z_sends.append(remote(block(0, dep), block(slot, dep), z_s.at[slot], z_r.at[slot], at_col((z + m + STEPS) % STEPS)))
    for cp in z_sends:
        cp.start()

    def to_core(s):
        return remote(block(s, dep), block(s, dep), cf_s.at[s], cf_r.at[s], at_depth(dep_c))

    def to_x(s):
        return remote(block(s, dep), block(s, dep), xf_s.at[s], xf_r.at[s], at_depth(dep_x))

    def x_to_core(s):
        return remote(block(s, dep_x), block(s, dep_x), cb_s.at[s], cb_r.at[s], at_depth(dep_c))

    def share(s):
        to_x(s).start()
        to_core(s).start()

    share(0)

    pick = (
        lax.broadcasted_iota(jnp.int32, (WIN, PAD), 0) - lax.broadcasted_iota(jnp.int32, (WIN, PAD), 1) == shift
    ) & (lax.broadcasted_iota(jnp.int32, (WIN, PAD), 1) < OWN)
    pick = jnp.where(pick, 1.0, 0.0).astype(BF16)
    for i in range(2):
        loads[2 + i].wait()

        def select(t, carry, i=i):
            r = pl.ds(pl.multiple_of(t * 224, 32), 224)
            cut = mm(win[i, r], pick).astype(BF16)
            for k in range(2):
                w2[k, r, i * 256 : (i + 1) * 256] = cut[:, k * 256 : (k + 1) * 256]
            return carry

        lax.fori_loop(0, 4, select, 0)
    loads[4].wait()
    wd[OWN:PAD, :] = jnp.zeros((PAD - OWN, WIDE), BF16)

    def y_send(s, j):
        d = (y + 4 - j) % 4
        return remote(psend.at[s, d], precv.at[s, j - 1], y_s.at[s, j - 1], y_r.at[s, j - 1], at_row(d, xh))

    def x_send(s):
        return remote(ysum.at[s, 1 - xh], xrecv.at[s], h_s.at[s], h_r.at[s], at_row(y, 1 - xh))

    def stage_products(s):
        to_core(s).wait_recv()
        x_to_core(s).wait_recv()
        xs = xd[0, s].reshape(DEEP * ROWS, WIDE)
        ds = xd[1, s].reshape(DEEP * ROWS, WIDE)
        for k in range(3):
            lanes = slice(k * PAD, (k + 1) * PAD)
            p = mm(xs, w2[k]) if k < 2 else mm_t(ds, wd[...])
            p = p.reshape(DEEP, ROWS, PAD)
            part[:, :, lanes] = p
            psend[s, :, :, lanes] = p.astype(BF16)
        for j in (2, 1, 3):
            y_send(s, j).start()
        part_own[s] = part[y]
        xt[:, :, pl.ds(pl.multiple_of(s * 128, 128), 128)] = xs.T.reshape(DEEP, PIECE, 128)

    def stage_y(s):
        total = part_own[s]
        for j in (1, 3, 2):
            y_send(s, j).wait_recv()
            total = total + precv[s, j - 1].astype(F32)
        ysum[s] = total.reshape(2, ROWS // 2, 3 * PAD)
        x_send(s).start()

    def stage_x(s):
        x_send(s).wait_recv()
        total = ysum[s, xh] + xrecv[s]
        for k in range(2):
            gate = total[:, k * PAD : k * PAD + 256]
            up = total[:, k * PAD + 256 : (k + 1) * PAD]
            back = total[:, 2 * PAD + k * 256 : 2 * PAD + (k + 1) * 256]
            sigma = jax.nn.sigmoid(gate)
            g[2, s, y, xh, :, k * 256 : (k + 1) * 256] = (gate * sigma * up).astype(BF16)
            g[k, s, y, xh, :, 0:256] = (back * up * sigma * (1.0 + gate * (1.0 - sigma))).astype(BF16)
            g[k, s, y, xh, :, 256:512] = (back * gate * sigma).astype(BF16)

    def step(it, carry):
        @pl.when((it >= 1) & (it < STEPS))
        def _():
            remote(block(0, dep), block(it, dep), z_s.at[it], z_r.at[it], at_col(z)).wait_recv()
            share(it)

        @pl.when((it >= 1) & (it < STEPS + 1))
        def _():
            s = it - 1
            to_x(s).wait_recv()
            x_to_core(s).start()

        @pl.when((it >= 2) & (it < STEPS + 2))
        def _():
            stage_products(it - 2)

        @pl.when((it >= 4) & (it < STEPS + 4))
        def _():
            stage_y(it - 4)

        @pl.when(it >= 5)
        def _():
            stage_x(it - 5)

        return carry

    lax.fori_loop(0, STEPS + 5, step, 0)

    def ag_x(k):
        return remote(g.at[k, :, y, xh], g.at[k, :, y, xh], ah_s.at[k], ah_r.at[k], at_row(y, 1 - xh))

    def ag_y(k, j):
        return remote(g.at[k, :, y, xh], g.at[k, :, y, xh], ay_s.at[k, j - 1], ay_r.at[k, j - 1], at_row((y + 4 - j) % 4, xh))

    def ag_f(k, j):
        src = g.at[k, :, y, 1 - xh]
        return remote(src, src, af_s.at[k, j - 1], af_r.at[k, j - 1], at_row((y + 4 - j) % 4, xh))

    for k in range(3):
        ag_x(k).start()
    for k in range(3):
        for j in (2, 1, 3):
            ag_y(k, j).start()
        ag_x(k).wait_recv()
        for j in (2, 1, 3):
            ag_f(k, j).start()

    def ag_wait(k):
        for j in (1, 2, 3):
            ag_y(k, j).wait_recv()
            ag_f(k, j).wait_recv()

    def piece(k, j):
        return remote(piece_send.at[k, j], piece_recv.at[k, j], p_s.at[k, j], p_r.at[k, j], at_depth((dep + j) % DEEP))

    for k in range(2):
        ag_wait(k)
        gk = g[k].reshape(1024, PAD)
        for j in (2, 1, 3, 0):
            rows = mm(xt[(dep + j) % DEEP], gk).astype(BF16)
            if j:
                piece_send[k, j] = rows
                piece(k, j).start()
            else:
                piece_recv[k, 0] = rows

    def ig_step(s, carry):
        r = mm_t(g[0, s].reshape(128, PAD), w2[0]) + mm_t(g[1, s].reshape(128, PAD), w2[1])
        r = r.reshape(2, 2, ROWS, WIDE)
        for a in range(2):
            for b in range(2):
                ig[b, a, s] = r[a, b]
        return carry

    lax.fori_loop(0, STEPS, ig_step, 0)
    ig_c = remote(ig.at[1 - c], ig_core, ic_s, ic_r, at_depth(dep_c))
    ig_c.start()

    ag_wait(2)

    def down_step(t, carry):
        lanes = pl.ds(pl.multiple_of(t * 128, 128), 128)
        h = g[2, :, :, :, :, lanes].reshape(1024, 128)
        r = lax.dot_general(h, xd[1].reshape(1024, WIDE), (((0,), (0,)), ((), ())), preferred_element_type=F32)
        down[pl.ds(pl.multiple_of(t * 128, 128), 128), :] = r.astype(BF16)
        return carry

    lax.fori_loop(0, 4, down_step, 0)
    down_copy = pltpu.make_async_copy(down.at[pl.ds(0, OWN)], down_out, out_sem.at[0])
    down_copy.start()

    ig_c.wait_recv()
    ig_xs[...] = (ig[c, 1 - xl] + ig_core[1 - xl]).astype(BF16)
    ig_x = remote(ig_xs, ig_xr, ix_s, ix_r, at_depth(dep_x))
    ig_x.start()
    ig_fin[...] = ig[c, xl] + ig_core[xl]
    ig_x.wait_recv()
    ig_fin[...] = ig_fin[...] + ig_xr[...].astype(F32)
    ig_zs[...] = ig_fin[...].astype(BF16)
    ig_sends = []
    for s in range(1, STEPS):
        cp = remote(ig_zs.at[s], ig_zr.at[s], iz_s.at[s], iz_r.at[s], at_col((z + DELTA[s] + STEPS) % STEPS))
        cp.start()
        ig_sends.append(cp)
    total = ig_fin[0]
    for s in range(1, STEPS):
        ig_sends[s - 1].wait_recv()
        total = total + ig_zr[s].astype(F32)
    ig_zs[0] = total.astype(BF16)
    ig_copy = pltpu.make_async_copy(ig_zs.at[0], ig_out, out_sem.at[1])
    ig_copy.start()

    for k in range(2):
        for j in (1, 2, 3):
            piece(k, j).wait_recv()
    gu_copies = []
    for k in range(2):
        for j in range(DEEP):
            src = (dep + DEEP - j) % DEEP
            gu_copies.append(pltpu.make_async_copy(piece_recv.at[k, j], gu_out.at[k, src], out_sem.at[2 + k * DEEP + j]))
    for cp in gu_copies:
        cp.start()

    for cp in z_sends:
        cp.wait_send()

    def drain(s, carry):
        to_core(s).wait_send()
        to_x(s).wait_send()
        x_to_core(s).wait_send()
        for j in (1, 2, 3):
            y_send(s, j).wait_send()
        x_send(s).wait_send()
        return carry

    lax.fori_loop(0, STEPS, drain, 0)
    for k in range(3):
        ag_x(k).wait_send()
        for j in (1, 2, 3):
            ag_y(k, j).wait_send()
            ag_f(k, j).wait_send()
    for k in range(2):
        for j in (1, 2, 3):
            piece(k, j).wait_send()
    ig_c.wait_send()
    ig_x.wait_send()
    for cp in ig_sends:
        cp.wait_send()
    down_copy.wait()
    ig_copy.wait()
    for cp in gu_copies:
        cp.wait()


def on_device(inputs, out_grad, w_gate, w_up, w_down):
    vm = pltpu.VMEM
    dma = pltpu.SemaphoreType.DMA
    anyspace = pl.BlockSpec(memory_space=pl.ANY)
    half = ROWS // 2
    ig, gu, down = pl.pallas_call(
        kernel,
        out_shape=(
            jax.ShapeDtypeStruct((ROWS, WIDE), BF16),
            jax.ShapeDtypeStruct((2, DEEP, PIECE, PAD), BF16),
            jax.ShapeDtypeStruct((OWN, WIDE), BF16),
        ),
        in_specs=[anyspace] * 5,
        out_specs=(anyspace,) * 3,
        scratch_shapes=[
            vm((2, STEPS, DEEP, ROWS, WIDE), BF16),
            vm((DEEP, PIECE, 1024), BF16),
            vm((2, WIDE, WIN), BF16),
            vm((2, WIDE, PAD), BF16),
            vm((PAD, WIDE), BF16),
            vm((DEEP, ROWS, 3 * PAD), F32),
            vm((STEPS, ROWS, 3 * PAD), F32),
            vm((STEPS, DEEP, ROWS, 3 * PAD), BF16),
            vm((STEPS, 3, ROWS, 3 * PAD), BF16),
            vm((STEPS, 2, half, 3 * PAD), F32),
            vm((STEPS, half, 3 * PAD), F32),
            vm((3, STEPS, 4, 2, half, PAD), BF16),
            vm((2, DEEP, PIECE, PAD), BF16),
            vm((2, DEEP, PIECE, PAD), BF16),
            vm((PAD, WIDE), BF16),
            vm((2, 2, STEPS, ROWS, WIDE), F32),
            vm((2, STEPS, ROWS, WIDE), F32),
            vm((STEPS, ROWS, WIDE), BF16),
            vm((STEPS, ROWS, WIDE), BF16),
            vm((STEPS, ROWS, WIDE), BF16),
            vm((STEPS, ROWS, WIDE), BF16),
            vm((STEPS, ROWS, WIDE), F32),
            dma((5,)),
            dma((8,)), dma((8,)),
            dma((8,)), dma((8,)),
            dma((8,)), dma((8,)),
            dma((8,)), dma((8,)),
            dma((8, 3)), dma((8, 3)),
            dma((8,)), dma((8,)),
            dma((3,)), dma((3,)),
            dma((3, 3)), dma((3, 3)),
            dma((3, 3)), dma((3, 3)),
            dma((2, 4)), dma((2, 4)),
            dma, dma,
            dma, dma,
            dma((8,)), dma((8,)),
            dma((10,)),
        ],
        compiler_params=pltpu.CompilerParams(
            collective_id=0, has_side_effects=True, vmem_limit_bytes=60 * 1024 * 1024
        ),
        cost_estimate=pl.CostEstimate(flops=8 * 10**9, bytes_accessed=12 * 10**6, transcendentals=10**6),
        name="ffn_backward",
    )(inputs, out_grad, w_gate, w_up, w_down)

    gu = gu.transpose(2, 1, 0, 3)
    gate = gu[..., :256].reshape(PIECE, DEEP, PAD)[..., :OWN].reshape(PIECE, FULL)
    up = gu[..., 256:].reshape(PIECE, DEEP, PAD)[..., :OWN].reshape(PIECE, FULL)
    return ig, gate, up, down


def solution(mesh):
    placed = (
        P(("depth", "col"), "row"),
        P(("depth", "col"), "row"),
        P("row", "col"),
        P("row", "col"),
        P("col", "row"),
    )
    return jax.shard_map(
        on_device,
        mesh=mesh,
        in_specs=placed,
        out_specs=(
            P(("depth", "col"), "row"),
            P(("row", "depth"), "col"),
            P(("row", "depth"), "col"),
            P(("col", "depth"), "row"),
        ),
        check_vma=False,
    )
```

time: 519 us -> 132 us (0.25)
  waiting for transfers between devices: 306 us -> 0 us
  blocking collectives: 141 us -> 0 us
  Pallas kernels: 0 us -> 122 us
  matrix products: 20.2 us -> 0 us
  local copies, waits for them, and re-layouts: 27.9 us -> 8.62 us
  between operations: 13.9 us -> 0.69 us
  other arithmetic: 8.86 us -> 0 us
    reduce_scatter x3 -> x0, waiting for transfers between devices: 180 us -> none  [the longest x1 111 us: on_device(): lax.psum_scatter(jnp.concatenate([gate_part, up_part, back_part], axis=1)...]
    all_gather x5 -> x0, blocking collectives: 141 us -> none  [the longest x1 32.9 us: on_device(): lax.all_gather(gate_back, 'row', axis=0, tiled=True)]
    unnamed x7 -> x0, waiting for transfers between devices: 126 us -> none
    pallas_call x0 -> x1, Pallas kernels: none -> 122 us  [on_device(): pl.pallas_call(kernel, out_shape=(jax.ShapeDtypeStruct((ROWS, WIDE), BF16...]
    unnamed x32 -> x7, local copies, waits for them, and re-layouts: 27.9 us -> 3.11 us
    dot_general x8 -> x0, matrix products: 20.2 us -> none  [the longest x3 12.9 us: contract_first(): lax.dot_general(left, right, (((0,), (0,)), ((), ())), preferred_element_...]
    convert_element_type x3 -> x0, other arithmetic: 5.95 us -> none  [the longest x1 2.45 us: on_device(): down_grad.astype(jnp.bfloat16)]
  transfers between devices with their start and end apart: 5 -> 0, of which waited for: 4 -> 0; matrix products, arithmetic and copies ran while one was open for 8% -> 0% of each run, Pallas kernels for 0% -> 0%
where the time goes in v1:
time: 132 us; the launch traced here: 131 us
  Pallas kernels  122 us (92%)
  local copies, waits for them, and re-layouts  8.62 us (7%)
    pallas_call x1, Pallas kernels, on_device(): pl.pallas_call(kernel, out_shape=(jax.ShapeDtypeStruct((ROWS, WIDE), BF16...  122 us
    unnamed x7, local copies, waits for them, and re-layouts  3.11 us

profile of v1, /device:TPU:1, one launch (start us, length us, event | category | flops | bytes accessed | tf_op | source)
XLA Modules:
  0.0 131.3 jit_solution(2759885419199215489)
XLA Ops:
  0.6 122.0 %ffn_backward.1 = (bf16[32,896]{1,0:T(8,128)(2,1)}, bf16[2,4,224,512]{3,2,1,0:T(8,128)(2,1)}, bf16[480,896]{1,0:T(8,128)(2,1)}) custom-call(bf16[32,896]{1,0:T(8,128)(2,1)} %x_hbm.1, bf16[32,896]{1,0:T(8,128)(2,1)} %dy_hbm.1, bf16[896,1920]{1,0:T(8,128)(2,1)} %wg_hbm.1, bf16[896,1920]{1,0:T(8,128)(2,1)} %wu_hbm.1, bf16[1920,896]{1,0:T(8,128)(2,1)} %wd_hbm.1), custom_call_target="tpu_custom_call" | custom-call | flops 8000000000 | bytes 12000000 | tf_op jit(solution)/shard_map/ffn_backward/pallas_call | solution.py:333
  122.6 1.6 %slice_bitcast_fusion = (bf16[2,4,28,8,256]{4,3,2,1,0:T(8,128)(2,1)S(1)}, bf16[2,4,28,8,256]{4,3,2,1,0:T(8,128)(2,1)S(1)}) fusion(bf16[224,4,2,512]{3,0,1,2:T(8,128)(2,1)} %bitcast.11), kind=kLoop, calls=%fused_computation | loop fusion | bytes 3670016
  124.2 0.1 copy.16
  124.2 0.7 copy.14
  125.0 0.0 copy-start.1
  125.0 0.0 copy-start
  125.0 2.0 %reshape.23 = bf16[224,1920]{1,0:T(8,128)(2,1)} reshape(bf16[224,4,480]{2,1,0:T(4,128)(2,1)S(1)} %copy.14) | data formatting | bytes 1720320 | tf_op jit(solution)/shard_map/reshape | solution.py:390
  127.0 0.1 copy.15
  127.0 0.7 copy.12
  127.8 2.0 %reshape.21 = bf16[224,1920]{1,0:T(8,128)(2,1)} reshape(bf16[224,4,480]{2,1,0:T(4,128)(2,1)S(1)} %copy.12) | data formatting | bytes 1720320 | tf_op jit(solution)/shard_map/reshape | solution.py:389
  129.7 0.0 copy-done.1
  129.7 0.6 copy.19
  130.4 0.0 copy-done
  130.4 0.9 copy.20
Async XLA Ops:
  125.0 4.8 %copy-start.1 = (bf16[32,896]{1,0:T(8,128)(2,1)S(1)}, bf16[32,896]{1,0:T(8,128)(2,1)}, u32[]{:S(2)}) copy-start(bf16[32,896]{1,0:T(8,128)(2,1)} %get-tuple-element.16) | copy-start | bytes 172036
  125.0 5.4 %copy-start = (bf16[480,896]{1,0:T(8,128)(2,1)S(1)}, bf16[480,896]{1,0:T(8,128)(2,1)}, u32[]{:S(2)}) copy-start(bf16[480,896]{1,0:T(8,128)(2,1)} %get-tuple-element.19) | copy-start | bytes 2580484

commit v2 on v0

v2 whole, which is shorter than its diff:
```python
import jax
import jax.numpy as jnp
from jax import lax
from jax.experimental import pallas as pl
from jax.experimental.pallas import tpu as pltpu
from jax.sharding import PartitionSpec as P

MESH = pl.DeviceIdType.MESH
F32, BF16 = jnp.float32, jnp.bfloat16

DELTA = (0, 1, -1, 2, -2, 3, -3, 4)
DEEP = 4
STEPS = 8
ROWS = 32
WIDE = 896
FULL = 1920
OWN = 480
PAD = 512
WIN = 640
PIECE = 224
HALF = ROWS // 2
CUT = 128
GU = 4
CHUNKS = 6
LANES = 2 * CUT
SUMS = 3 * PAD
GROUPS = ((0, 1), (1, 3), (3, 5), (5, 7), (7, 8))
PARTS = tuple((k, 0, 5) for k in range(4)) + tuple((k, 5, 8) for k in range(4)) + ((4, 0, 8), (5, 0, 8))


def mm(a, b):
    return lax.dot_general(a, b, (((1,), (0,)), ((), ())), preferred_element_type=F32)


def mm_t(a, b):
    return lax.dot_general(a, b, (((1,), (1,)), ((), ())), preferred_element_type=F32)


def kernel(
    x_hbm, dy_hbm, wg_hbm, wu_hbm, wd_hbm,
    ig_out, gate_out, up_out, down_out,
    xd, xt, win, w2, w2t, wd, part, part_own, psend, precv, ysum, xrecv, g,
    piece_send, piece_recv, gate_fin, up_fin, down, ig, ig_core, ig_xs, ig_xr, ig_zs, ig_zr, ig_fin, ig_res,
    load_sem, zo_s, zo_r, zf_s, zf_r, co_s, co_r, cf_s, cf_r, x0_s, x0_r, y_s, y_r, h_s, h_r,
    ah_s, ah_r, ay_s, ay_r, af_s, af_r, p_s, p_r, ic_s, ic_r, ix_s, ix_r, iz_s, iz_r, out_sem,
):
    row, z, dep = lax.axis_index("row"), lax.axis_index("col"), lax.axis_index("depth")
    y, xh = row // 2, row % 2
    xl, c = dep // 2, dep % 2
    dep_x = (1 - xl) * 2 + c
    dep_c = xl * 2 + 1 - c
    dep_xc = (1 - xl) * 2 + 1 - c
    y_up, y_down = (y + 1) % 4, (y + 3) % 4

    def at_row(yy, hh):
        return {"row": yy * 2 + hh, "col": z, "depth": dep}

    def at_depth(d):
        return {"row": row, "col": z, "depth": d}

    def at_col(zz):
        return {"row": row, "col": zz, "depth": dep}

    x_peer = at_row(y, 1 - xh)

    def remote(src, dst, ss, rs, dev):
        return pltpu.make_async_remote_copy(
            src_ref=src, dst_ref=dst, send_sem=ss, recv_sem=rs, device_id=dev, device_id_type=MESH
        )

    start = jnp.where(dep == 3, 1280, dep * 480 - (dep * 480) % 128)
    start = pl.multiple_of(start, 128)
    shift = dep * 480 - start
    loads = [
        pltpu.make_async_copy(x_hbm, xd.at[0, 0, xl, c], load_sem.at[0]),
        pltpu.make_async_copy(dy_hbm, xd.at[1, 0, xl, c], load_sem.at[1]),
        pltpu.make_async_copy(wg_hbm.at[:, pl.ds(start, WIN)], win.at[0], load_sem.at[2]),
        pltpu.make_async_copy(wu_hbm.at[:, pl.ds(start, WIN)], win.at[1], load_sem.at[3]),
        pltpu.make_async_copy(wd_hbm.at[pl.ds(dep * OWN, OWN)], wd.at[pl.ds(0, OWN)], load_sem.at[4]),
    ]
    for cp in loads:
        cp.start()

    barrier = pltpu.get_barrier_semaphore()
    peers = [at_depth(dep_x), at_depth(dep_c), at_depth(dep_xc)]
    peers += [at_col((z + m) % STEPS) for m in range(1, STEPS)]
    peers += [at_row((y + m) % 4, xh) for m in (1, 2, 3)] + [x_peer]
    peers += [{"row": row, "col": (z + m) % STEPS, "depth": dep_x} for m in (1, STEPS - 1)]
    for dev in peers:
        pl.semaphore_signal(barrier, inc=1, device_id=dev, device_id_type=MESH)

    pick = (
        lax.broadcasted_iota(jnp.int32, (WIN, PAD), 0) - lax.broadcasted_iota(jnp.int32, (WIN, PAD), 1) == shift
    ) & (lax.broadcasted_iota(jnp.int32, (WIN, PAD), 1) < OWN)
    pick = jnp.where(pick, 1.0, 0.0).astype(BF16)

    def select(i):
        loads[2 + i].wait()

        def one(t, carry):
            r = pl.ds(pl.multiple_of(t * 224, 32), 224)
            cut = mm(win[i, r], pick).astype(BF16)
            for k in range(GU):
                w2[r, k * LANES + i * CUT : k * LANES + (i + 1) * CUT] = cut[:, k * CUT : (k + 1) * CUT]
            return carry

        lax.fori_loop(0, 4, one, 0)

    select(0)
    loads[0].wait()
    loads[1].wait()
    pl.semaphore_wait(barrier, len(peers))

    def block(s, a, b):
        return xd.at[:, s, a, b]

    def ring(s, a, ss, rs):
        to = (z + STEPS - 1) % STEPS if s % 2 else (z + 1) % STEPS
        return remote(block(max(s - 2, 0), a, c), block(s, a, c), ss.at[s], rs.at[s], at_col(to))

    def ring_last(a, ss, rs, i):
        to = (z + 1) % STEPS if i == 0 else (z + STEPS - 1) % STEPS
        src = 6 if i == 0 else 5
        return remote(xd.at[i, src, a, c], xd.at[i, 7, a, c], ss.at[7 + i], rs.at[7 + i], at_col(to))

    def to_core(s, a, ss, rs):
        return remote(block(s, a, c), block(s, a, c), ss.at[s], rs.at[s], at_depth(dep_c))

    def to_x():
        return remote(block(0, xl, c), block(0, xl, c), x0_s, x0_r, at_depth(dep_x))

    def diagonal(s):
        to = (z + STEPS - 1) % STEPS if s == 1 else (z + 1) % STEPS
        dev = {"row": row, "col": to, "depth": dep_x}
        return remote(block(0, xl, c), block(s, xl, c), zf_s.at[s], zf_r.at[s], dev)

    to_x().start()
    ring(1, xl, zo_s, zo_r).start()
    ring(2, xl, zo_s, zo_r).start()
    diagonal(1).start()
    diagonal(2).start()
    to_core(0, xl, co_s, co_r).start()

    select(1)
    loads[4].wait()
    wd[OWN:PAD, :] = jnp.zeros((PAD - OWN, WIDE), BF16)

    def arrive_pair(m, a, zs, zr, cs, cr):
        for s in (2 * m - 1, 2 * m):
            ring(s, a, zs, zr).wait_recv()
            if m < 3:
                ring(s + 2, a, zs, zr).start()
            else:
                ring_last(a, zs, zr, s % 2).start()
        for s in (2 * m - 1, 2 * m):
            to_core(s, a, cs, cr).start()

    def arrive_last(a, zs, zr, cs, cr):
        ring_last(a, zs, zr, 0).wait_recv()
        ring_last(a, zs, zr, 1).wait_recv()
        to_core(7, a, cs, cr).start()

    own_sems = (zo_s, zo_r, co_s, co_r)
    far_sems = (zf_s, zf_r, cf_s, cf_r)

    def y_send(q, j):
        d = (y + 4 - j) % 4
        rows = pl.ds(GROUPS[q][0], GROUPS[q][1] - GROUPS[q][0])
        return remote(psend.at[d, rows], precv.at[j - 1, rows], y_s.at[q, j - 1], y_r.at[q, j - 1], at_row(d, xh))

    def x_send(q):
        rows = pl.ds(GROUPS[q][0], GROUPS[q][1] - GROUPS[q][0])
        return remote(ysum.at[1 - xh, rows], xrecv.at[rows], h_s.at[q], h_r.at[q], x_peer)

    def ag_x(q):
        lo, hi = GROUPS[q]
        rows = g.at[:, lo:hi, y, xh]
        return remote(rows, rows, ah_s.at[q], ah_r.at[q], x_peer)

    def ag_x_wait(q):
        lo, hi = GROUPS[q]
        rows = g.at[:, lo:hi, y, 1 - xh]
        remote(rows, rows, ah_s.at[q], ah_r.at[q], x_peer).wait_recv()

    def stage_products(q):
        lo, hi = GROUPS[q]
        n = hi - lo
        for s in range(lo, hi):
            to_core(s, xl, co_s, co_r).wait_recv()
            to_core(s, 1 - xl, cf_s, cf_r).wait_recv()
        xs = xd[0, lo:hi].reshape(n * 128, WIDE)
        ds = xd[1, lo:hi].reshape(n * 128, WIDE)
        for a, b, p in ((0, 2 * PAD, mm(xs, w2[...])), (2 * PAD, SUMS, mm_t(ds, wd[...]))):
            p = p.reshape(n, DEEP, ROWS, b - a)
            for s in range(n):
                part[:, s, :, a:b] = p[s]
                psend[:, lo + s, :, a:b] = p[s].astype(BF16)
        for j in (2, 1, 3):
            y_send(q, j).start()
        part_own[lo:hi] = part[y, 0:n]
        for s in range(lo, hi):
            xt[:, :, s * 128 : (s + 1) * 128] = xd[0, s].reshape(128, WIDE).T.reshape(DEEP, PIECE, 128)

    def stage_y(q):
        lo, hi = GROUPS[q]
        for j in (1, 3, 2):
            y_send(q, j).wait_recv()
        for s in range(lo, hi):
            total = part_own[s]
            for j in (1, 3, 2):
                total = total + precv[j - 1, s].astype(F32)
            total = total.reshape(2, HALF, SUMS)
            ysum[0, s] = total[0]
            ysum[1, s] = total[1]
        x_send(q).start()

    def stage_x(q):
        lo, hi = GROUPS[q]
        x_send(q).wait_recv()
        for s in range(lo, hi):
            total = ysum[xh, s] + xrecv[s]
            for k in range(GU):
                gate = total[:, k * LANES : k * LANES + CUT]
                up = total[:, k * LANES + CUT : (k + 1) * LANES]
                back = total[:, 2 * PAD + k * CUT : 2 * PAD + (k + 1) * CUT]
                sigma = jax.nn.sigmoid(gate)
                lanes = slice((k % 2) * CUT, (k % 2 + 1) * CUT)
                g[GU + k // 2, s, y, xh, :, lanes] = (gate * sigma * up).astype(BF16)
                g[k, s, y, xh, :, 0:CUT] = (back * up * sigma * (1.0 + gate * (1.0 - sigma))).astype(BF16)
                g[k, s, y, xh, :, CUT:LANES] = (back * gate * sigma).astype(BF16)
        ag_x(q).start()

    def ag_own(p, up):
        k, lo, hi = PARTS[p]
        rows = g.at[k, lo:hi, y]
        i = 0 if up else 1
        return remote(rows, rows, ay_s.at[p, i], ay_r.at[p, i], at_row(y_up if up else y_down, xh))

    def ag_own_wait(p, up):
        k, lo, hi = PARTS[p]
        rows = g.at[k, lo:hi, y_down if up else y_up]
        i = 0 if up else 1
        remote(rows, rows, ay_s.at[p, i], ay_r.at[p, i], at_row(y_up, xh)).wait_recv()

    def ag_pass(p, up):
        k, lo, hi = PARTS[p]
        i = 0 if up else 1
        rows = g.at[k, lo:hi, y_down if up else y_up, i]
        return remote(rows, rows, af_s.at[p, i], af_r.at[p, i], at_row(y_up if up else y_down, xh))

    def ag_pass_wait(p, up):
        k, lo, hi = PARTS[p]
        i = 0 if up else 1
        rows = g.at[k, lo:hi, (y + 2) % 4, i]
        remote(rows, rows, af_s.at[p, i], af_r.at[p, i], at_row(y_up, xh)).wait_recv()

    def ag_start(p):
        for up in (True, False):
            ag_own(p, up).start()

    def ag_middle(p):
        for up in (True, False):
            ag_own_wait(p, up)
            ag_pass(p, up).start()

    def ag_end(p):
        for up in (True, False):
            ag_pass_wait(p, up)

    src = block(0, 1 - xl, c)
    remote(src, src, x0_s, x0_r, at_depth(dep_x)).wait_recv()
    to_core(0, 1 - xl, cf_s, cf_r).start()
    arrive_pair(1, xl, *own_sems)
    stage_products(0)
    arrive_pair(1, 1 - xl, *far_sems)
    arrive_pair(2, xl, *own_sems)
    stage_products(1)
    arrive_pair(2, 1 - xl, *far_sems)
    arrive_pair(3, xl, *own_sems)
    stage_y(0)
    stage_products(2)
    arrive_pair(3, 1 - xl, *far_sems)
    arrive_last(xl, *own_sems)
    stage_x(0)
    stage_products(3)
    stage_y(1)
    arrive_last(1 - xl, *far_sems)
    stage_products(4)
    stage_x(1)
    stage_y(2)
    for k in range(GU):
        w2t[k * LANES : (k + 1) * LANES, :] = w2[:, k * LANES : (k + 1) * LANES].T
    stage_x(2)
    stage_y(3)
    for q in range(3):
        ag_x_wait(q)
    for p in range(4):
        ag_start(p)
    stage_x(3)
    stage_y(4)
    for p in range(4):
        ag_middle(p)
    stage_x(4)
    for q in (3, 4):
        ag_x_wait(q)

    def piece(k, j):
        d = (dep + j) % DEEP
        return remote(piece_send.at[k, d], piece_recv.at[k, dep], p_s.at[k, j], p_r.at[k, j], at_depth(d))

    def piece_wait(k, j):
        dst = piece_recv.at[k, (dep + DEEP - j) % DEEP]
        remote(dst, dst, p_s.at[k, j], p_r.at[k, j], at_depth(dep_x)).wait_recv()

    def pieces(k):
        gk = g[k].reshape(1024, LANES)
        piece_send[k] = mm(xt[...].reshape(WIDE, 1024), gk).astype(BF16).reshape(DEEP, PIECE, LANES)

    def pieces_start(k):
        for j in (2, 1, 3):
            piece(k, j).start()
        piece_recv[k, dep] = piece_send[k, dep]

    def ig_group(q):
        lo, hi = GROUPS[q]
        r = 0.0
        for k in range(GU):
            r = r + mm(g[k, lo:hi].reshape((hi - lo) * 128, LANES), w2t[k * LANES : (k + 1) * LANES, :])
        r = r.reshape(hi - lo, 2, 2, ROWS, WIDE)
        for s in range(lo, hi):
            for a in range(2):
                for b in range(2):
                    ig[b, a, s] = r[s - lo, a, b]
        ig_c(q).start()

    def ig_c(q):
        lo, hi = GROUPS[q]
        return remote(ig.at[1 - c, :, lo:hi], ig_core.at[:, lo:hi], ic_s.at[q], ic_r.at[q], at_depth(dep_c))

    def ig_z(s):
        return remote(ig_zs.at[s], ig_zr.at[s], iz_s.at[s], iz_r.at[s], at_col((z + DELTA[s] + STEPS) % STEPS))

    def ig_chip(q):
        lo, hi = GROUPS[q]
        ig_c(q).wait_recv()
        for s in range(lo, hi):
            total = ig[c, :, s] + ig_core[:, s]
            if s:
                ig_zs[s] = total.astype(BF16)
                ig_z(s).start()
            else:
                ig_fin[...] = total

    for p in range(4, 8):
        ag_start(p)
    for p in range(4):
        ag_end(p)
    for q in (2, 1, 0):
        ig_group(q)
    ag_middle(4)
    ag_start(8)
    ag_middle(5)
    ag_start(9)
    ig_chip(2)
    ag_middle(6)
    ag_middle(7)
    ag_end(4)
    pieces(0)
    pieces_start(0)
    ig_chip(1)
    ig_chip(0)
    ag_end(5)
    pieces(1)
    pieces_start(1)
    ag_end(6)
    ag_end(7)
    ig_group(4)
    ig_group(3)
    ag_middle(8)
    ag_middle(9)
    pieces(2)
    pieces_start(2)
    ig_chip(4)
    ig_chip(3)
    pieces(3)
    pieces_start(3)

    ag_end(8)
    ag_end(9)

    def down_step(t, carry):
        h = g[GU + t].reshape(1024, LANES)
        r = lax.dot_general(h, xd[1].reshape(1024, WIDE), (((0,), (0,)), ((), ())), preferred_element_type=F32)
        down[pl.ds(pl.multiple_of(t * LANES, LANES), LANES), :] = r.astype(BF16)
        return carry

    lax.fori_loop(0, 2, down_step, 0)
    outs = [pltpu.make_async_copy(down.at[pl.ds(0, OWN)], down_out, out_sem.at[0])]
    outs[0].start()

    def assemble(k):
        for j in (1, 2, 3):
            piece_wait(k, j)
        wide = min(CUT, OWN - k * CUT)
        for src in range(DEEP):
            lanes = slice(src * OWN + k * CUT, src * OWN + k * CUT + wide)
            gate_fin[:, lanes] = piece_recv[k, src, :, 0:wide]
            up_fin[:, lanes] = piece_recv[k, src, :, CUT : CUT + wide]

    assemble(0)
    assemble(1)
    total = ig_fin[...]
    for s in range(1, STEPS):
        ig_z(s).wait_recv()
        total = total + ig_zr[s].astype(F32)
    ig_fin[...] = total

    ig_xs[...] = ig_fin[1 - xl].astype(BF16)
    ig_x = remote(ig_xs, ig_xr, ix_s, ix_r, at_depth(dep_x))
    ig_x.start()
    assemble(2)
    ig_x.wait_recv()
    ig_res[...] = (ig_fin[xl] + ig_xr[...].astype(F32)).astype(BF16)
    outs.append(pltpu.make_async_copy(ig_res, ig_out, out_sem.at[3]))
    outs[-1].start()
    assemble(3)
    for i, (src, dst) in enumerate(((gate_fin, gate_out), (up_fin, up_out))):
        outs.append(pltpu.make_async_copy(src, dst, out_sem.at[1 + i]))
        outs[-1].start()

    to_x().wait_send()
    diagonal(1).wait_send()
    diagonal(2).wait_send()
    for a, zs, zr, cs, cr in ((xl, *own_sems), (1 - xl, *far_sems)):
        ring_last(a, zs, zr, 0).wait_send()
        ring_last(a, zs, zr, 1).wait_send()

        for s in range(1 if zs is zo_s else 3, 7):
            ring(s, a, zs, zr).wait_send()
        for s in range(STEPS):
            to_core(s, a, cs, cr).wait_send()

    for q in range(len(GROUPS)):
        for j in (1, 2, 3):
            y_send(q, j).wait_send()
        x_send(q).wait_send()
        ag_x(q).wait_send()
    for p in range(len(PARTS)):
        for up in (True, False):
            ag_own(p, up).wait_send()
            ag_pass(p, up).wait_send()
    for k in range(GU):
        for j in (1, 2, 3):
            piece(k, j).wait_send()
    for q in range(len(GROUPS)):
        ig_c(q).wait_send()
    ig_x.wait_send()
    for s in range(1, STEPS):
        ig_z(s).wait_send()
    for cp in outs:
        cp.wait()


def hand_on(a0, a1, a2, a3, b0, b1, b2, b3, sems):
    copies = [
        pltpu.make_async_copy(a, b, sems.at[i]) for i, (a, b) in enumerate(((a0, b0), (a1, b1), (a2, b2), (a3, b3)))
    ]
    for cp in copies:
        cp.start()
    for cp in copies:
        cp.wait()


def on_device(inputs, out_grad, w_gate, w_up, w_down):
    vm = pltpu.VMEM
    dma = pltpu.SemaphoreType.DMA
    anyspace = pl.BlockSpec(memory_space=pl.ANY)
    shapes = (
        jax.ShapeDtypeStruct((ROWS, WIDE), BF16),
        jax.ShapeDtypeStruct((PIECE, FULL), BF16),
        jax.ShapeDtypeStruct((PIECE, FULL), BF16),
        jax.ShapeDtypeStruct((OWN, WIDE), BF16),
    )
    results = pl.pallas_call(
        kernel,
        out_shape=shapes,
        in_specs=[anyspace] * 5,
        out_specs=(anyspace,) * 4,
        scratch_shapes=[
            vm((2, STEPS, 2, 2, ROWS, WIDE), BF16),
            vm((DEEP, PIECE, 1024), BF16),
            vm((2, WIDE, WIN), BF16),
            vm((WIDE, 2 * PAD), BF16),
            vm((2 * PAD, WIDE), BF16),
            vm((PAD, WIDE), BF16),
            vm((DEEP, 2, ROWS, SUMS), F32),
            vm((STEPS, ROWS, SUMS), F32),
            vm((DEEP, STEPS, ROWS, SUMS), BF16),
            vm((3, STEPS, ROWS, SUMS), BF16),
            vm((2, STEPS, HALF, SUMS), F32),
            vm((STEPS, HALF, SUMS), F32),
            vm((CHUNKS, STEPS, 4, 2, HALF, LANES), BF16),
            vm((GU, DEEP, PIECE, LANES), BF16),
            vm((GU, DEEP, PIECE, LANES), BF16),
            vm((PIECE, FULL), BF16),
            vm((PIECE, FULL), BF16),
            vm((PAD, WIDE), BF16),
            vm((2, 2, STEPS, ROWS, WIDE), F32),
            vm((2, STEPS, ROWS, WIDE), F32),
            vm((ROWS, WIDE), BF16),
            vm((ROWS, WIDE), BF16),
            vm((STEPS, 2, ROWS, WIDE), BF16),
            vm((STEPS, 2, ROWS, WIDE), BF16),
            vm((2, ROWS, WIDE), F32),
            vm((ROWS, WIDE), BF16),
            dma((5,)),
            dma((9,)), dma((9,)),
            dma((9,)), dma((9,)),
            dma((8,)), dma((8,)),
            dma((8,)), dma((8,)),
            dma, dma,
            dma((5, 3)), dma((5, 3)),
            dma((5,)), dma((5,)),
            dma((5,)), dma((5,)),
            dma((10, 2)), dma((10, 2)),
            dma((10, 2)), dma((10, 2)),
            dma((GU, 4)), dma((GU, 4)),
            dma((5,)), dma((5,)),
            dma, dma,
            dma((8,)), dma((8,)),
            dma((4,)),
        ],
        compiler_params=pltpu.CompilerParams(
            collective_id=0, has_side_effects=True, vmem_limit_bytes=60 * 1024 * 1024
        ),
        cost_estimate=pl.CostEstimate(flops=8 * 10**9, bytes_accessed=12 * 10**6, transcendentals=10**6),
        name="ffn_backward",
    )(inputs, out_grad, w_gate, w_up, w_down)
    return pl.pallas_call(
        hand_on,
        out_shape=shapes,
        in_specs=[pl.BlockSpec(memory_space=pltpu.VMEM)] * 4,
        out_specs=(anyspace,) * 4,
        scratch_shapes=[dma((4,))],
        name="hand_on",
    )(*results)


def solution(mesh):
    placed = (
        P(("depth", "col"), "row"),
        P(("depth", "col"), "row"),
        P("row", "col"),
        P("row", "col"),
        P("col", "row"),
    )
    return jax.shard_map(
        on_device,
        mesh=mesh,
        in_specs=placed,
        out_specs=(
            P(("depth", "col"), "row"),
            P(("row", "depth"), "col"),
            P(("row", "depth"), "col"),
            P(("col", "depth"), "row"),
        ),
        check_vma=False,
    )
```

time: 519 us -> 111 us (0.21)
  waiting for transfers between devices: 306 us -> 0 us
  blocking collectives: 141 us -> 0 us
  Pallas kernels: 0 us -> 109 us
  local copies, waits for them, and re-layouts: 27.9 us -> 0 us
  matrix products: 20.2 us -> 0 us
  between operations: 13.9 us -> 0.64 us
  other arithmetic: 8.86 us -> 0 us
    reduce_scatter x3 -> x0, waiting for transfers between devices: 180 us -> none  [the longest x1 111 us: on_device(): lax.psum_scatter(jnp.concatenate([gate_part, up_part, back_part], axis=1)...]
    all_gather x5 -> x0, blocking collectives: 141 us -> none  [the longest x1 32.9 us: on_device(): lax.all_gather(gate_back, 'row', axis=0, tiled=True)]
    unnamed x7 -> x0, waiting for transfers between devices: 126 us -> none
    pallas_call x0 -> x2, Pallas kernels: none -> 109 us  [the longest x1 106 us: on_device(): pl.pallas_call(kernel, out_shape=shapes, in_specs=[anyspace] * 5, out_spe...]
    unnamed x32 -> x0, local copies, waits for them, and re-layouts: 27.9 us -> none
    dot_general x8 -> x0, matrix products: 20.2 us -> none  [the longest x3 12.9 us: contract_first(): lax.dot_general(left, right, (((0,), (0,)), ((), ())), preferred_element_...]
    convert_element_type x3 -> x0, other arithmetic: 5.95 us -> none  [the longest x1 2.45 us: on_device(): down_grad.astype(jnp.bfloat16)]
  transfers between devices with their start and end apart: 5 -> 0, of which waited for: 4 -> 0; matrix products, arithmetic and copies ran while one was open for 8% -> 0% of each run, Pallas kernels for 0% -> 0%
where the time goes in v2:
time: 111 us; the launch traced here: 110 us
  Pallas kernels  109 us (98%)
    pallas_call x1, Pallas kernels, on_device(): pl.pallas_call(kernel, out_shape=shapes, in_specs=[anyspace] * 5, out_spe...  106 us
    pallas_call x1, Pallas kernels, on_device(): pl.pallas_call(hand_on, out_shape=shapes, in_specs=[pl.BlockSpec(memory_s...  3.22 us

profile of v2, /device:TPU:1, one launch (start us, length us, event | category | flops | bytes accessed | tf_op | source)
XLA Modules:
  0.0 109.6 jit_solution(10170385805533221493)
XLA Ops:
  0.6 105.7 %ffn_backward.1 = (bf16[32,896]{1,0:T(8,128)(2,1)}, bf16[224,1920]{1,0:T(8,128)(2,1)}, bf16[224,1920]{1,0:T(8,128)(2,1)}, bf16[480,896]{1,0:T(8,128)(2,1)}) custom-call(bf16[32,896]{1,0:T(8,128)(2,1)} %x_hbm.1, bf16[32,896]{1,0:T(8,128)(2,1)} %dy_hbm.1, bf16[896,1920]{1,0:T(8,128)(2,1)} %wg_hbm.1, bf16[896,1920]{1,0:T(8,128)(2,1)} %wu_hbm.1, ...), custom_call_target="tpu_custom_call" | custom-call | flops 8000000000 | bytes 12000000 | tf_op jit(solution)/shard_map/ffn_backward/pallas_call | solution.py:484
  106.3 3.2 %hand_on.1 = (bf16[32,896]{1,0:T(8,128)(2,1)}, bf16[224,1920]{1,0:T(8,128)(2,1)}, bf16[224,1920]{1,0:T(8,128)(2,1)}, bf16[480,896]{1,0:T(8,128)(2,1)}) custom-call(bf16[32,896]{1,0:T(8,128)(2,1)} %get-tuple-element.8.a0, bf16[224,1920]{1,0:T(8,128)(2,1)} %get-tuple-element.9.a1, bf16[224,1920]{1,0:T(8,128)(2,1)} %get-tuple-element.10.a2, ...), custom_call_target="tpu_custom_call" | custom-call | tf_op jit(solution)/shard_map/hand_on/pallas_call | solution.py:539

commit v3 on v2

--- a/solution.py
+++ b/solution.py
@@ -298,9 +298,9 @@
         ag_start(p)
     stage_x(3)
     stage_y(4)
+    stage_x(4)
     for p in range(4):
         ag_middle(p)
-    stage_x(4)
     for q in (3, 4):
         ag_x_wait(q)
 
@@ -355,35 +355,36 @@
         ag_start(p)
     for p in range(4):
         ag_end(p)
-    for q in (2, 1, 0):
-        ig_group(q)
+    ig_group(2)
     ag_middle(4)
-    ag_start(8)
     ag_middle(5)
-    ag_start(9)
-    ig_chip(2)
+    ig_group(1)
     ag_middle(6)
     ag_middle(7)
+    ag_start(8)
+    ag_start(9)
     ag_end(4)
     pieces(0)
     pieces_start(0)
-    ig_chip(1)
-    ig_chip(0)
+    ig_chip(2)
+    ig_group(0)
     ag_end(5)
     pieces(1)
     pieces_start(1)
+    ig_chip(1)
+    ig_chip(0)
     ag_end(6)
     ag_end(7)
     ig_group(4)
     ig_group(3)
-    ag_middle(8)
-    ag_middle(9)
     pieces(2)
     pieces_start(2)
     ig_chip(4)
     ig_chip(3)
     pieces(3)
     pieces_start(3)
+    ag_middle(8)
+    ag_middle(9)
 
     ag_end(8)
     ag_end(9)
@@ -461,13 +462,16 @@
         cp.wait()
 
 
-def hand_on(a0, a1, a2, a3, b0, b1, b2, b3, sems):
-    copies = [
-        pltpu.make_async_copy(a, b, sems.at[i]) for i, (a, b) in enumerate(((a0, b0), (a1, b1), (a2, b2), (a3, b3)))
-    ]
-    for cp in copies:
+def hand_on(a0, a1, a2, a3, b0, b1, b2, b3, v0, v1, v2, v3, sem_in, sem_out):
+    sets = ((a1, v1, b1), (a2, v2, b2), (a3, v3, b3), (a0, v0, b0))
+    loads = [pltpu.make_async_copy(a, v, sem_in.at[i]) for i, (a, v, b) in enumerate(sets)]
+    stores = [pltpu.make_async_copy(v, b, sem_out.at[i]) for i, (a, v, b) in enumerate(sets)]
+    for cp in loads:
         cp.start()
-    for cp in copies:
+    for load, store in zip(loads, stores):
+        load.wait()
+        store.start()
+    for cp in stores:
         cp.wait()
 
 
@@ -539,9 +543,9 @@
     return pl.pallas_call(
         hand_on,
         out_shape=shapes,
-        in_specs=[pl.BlockSpec(memory_space=pltpu.VMEM)] * 4,
+        in_specs=[anyspace] * 4,
         out_specs=(anyspace,) * 4,
-        scratch_shapes=[dma((4,))],
+        scratch_shapes=[vm(a.shape, BF16) for a in shapes] + [dma((4,)), dma((4,))],
         name="hand_on",
     )(*results)
 

time: 111 us -> 108 us (0.973)
  Pallas kernels: 109 us -> 107 us
    pallas_call x1, Pallas kernels: 106 us -> 104 us  [on_device(): pl.pallas_call(kernel, out_shape=shapes, in_specs=[anyspace] * 5, out_spe...]
where the time goes in v3:
time: 108 us
  Pallas kernels  107 us (99%)
    pallas_call x1, Pallas kernels, on_device(): pl.pallas_call(kernel, out_shape=shapes, in_specs=[anyspace] * 5, out_spe...  104 us
    pallas_call x1, Pallas kernels, on_device(): pl.pallas_call(hand_on, out_shape=shapes, in_specs=[anyspace] * 4, out_sp...  2.7 us

profile of v3, /device:TPU:1, one launch (start us, length us, event | category | flops | bytes accessed | tf_op | source)
XLA Modules:
  0.0 107.6 jit_solution(3875978615894263728)
XLA Ops:
  0.6 104.2 %ffn_backward.1 = (bf16[32,896]{1,0:T(8,128)(2,1)}, bf16[224,1920]{1,0:T(8,128)(2,1)}, bf16[224,1920]{1,0:T(8,128)(2,1)}, bf16[480,896]{1,0:T(8,128)(2,1)}) custom-call(bf16[32,896]{1,0:T(8,128)(2,1)} %x_hbm.1, bf16[32,896]{1,0:T(8,128)(2,1)} %dy_hbm.1, bf16[896,1920]{1,0:T(8,128)(2,1)} %wg_hbm.1, bf16[896,1920]{1,0:T(8,128)(2,1)} %wu_hbm.1, ...), custom_call_target="tpu_custom_call" | custom-call | flops 8000000000 | bytes 12000000 | tf_op jit(solution)/shard_map/ffn_backward/pallas_call | solution.py:488
  104.9 2.7 %hand_on.1 = (bf16[32,896]{1,0:T(8,128)(2,1)}, bf16[224,1920]{1,0:T(8,128)(2,1)}, bf16[224,1920]{1,0:T(8,128)(2,1)}, bf16[480,896]{1,0:T(8,128)(2,1)}) custom-call(bf16[32,896]{1,0:T(8,128)(2,1)} %get-tuple-element.8.a0, bf16[224,1920]{1,0:T(8,128)(2,1)} %get-tuple-element.9.a1, bf16[224,1920]{1,0:T(8,128)(2,1)} %get-tuple-element.10.a2, ...), custom_call_target="tpu_custom_call" | custom-call | tf_op jit(solution)/shard_map/hand_on/pallas_call | solution.py:543

commit v4 on v3

--- a/solution.py
+++ b/solution.py
@@ -106,7 +106,6 @@
 
         lax.fori_loop(0, 4, one, 0)
 
-    select(0)
     loads[0].wait()
     loads[1].wait()
     pl.semaphore_wait(barrier, len(peers))
@@ -141,6 +140,7 @@
     diagonal(2).start()
     to_core(0, xl, co_s, co_r).start()
 
+    select(0)
     select(1)
     loads[4].wait()
     wd[OWN:PAD, :] = jnp.zeros((PAD - OWN, WIDE), BF16)
@@ -174,13 +174,17 @@
 
     def ag_x(q):
         lo, hi = GROUPS[q]
-        rows = g.at[:, lo:hi, y, xh]
+        rows = g.at[0:GU, lo:hi, y, xh]
         return remote(rows, rows, ah_s.at[q], ah_r.at[q], x_peer)
 
     def ag_x_wait(q):
         lo, hi = GROUPS[q]
-        rows = g.at[:, lo:hi, y, 1 - xh]
+        rows = g.at[0:GU, lo:hi, y, 1 - xh]
         remote(rows, rows, ah_s.at[q], ah_r.at[q], x_peer).wait_recv()
+
+    def ag_x_hidden(half):
+        rows = g.at[GU:CHUNKS, :, y, half]
+        return remote(rows, rows, ah_s.at[5], ah_r.at[5], x_peer)
 
     def stage_products(q):
         lo, hi = GROUPS[q]
@@ -299,6 +303,7 @@
     stage_x(3)
     stage_y(4)
     stage_x(4)
+    ag_x_hidden(xh).start()
     for p in range(4):
         ag_middle(p)
     for q in (3, 4):
@@ -361,6 +366,7 @@
     ig_group(1)
     ag_middle(6)
     ag_middle(7)
+    ag_x_hidden(1 - xh).wait_recv()
     ag_start(8)
     ag_start(9)
     ag_end(4)
@@ -408,7 +414,29 @@
             gate_fin[:, lanes] = piece_recv[k, src, :, 0:wide]
             up_fin[:, lanes] = piece_recv[k, src, :, CUT : CUT + wide]
 
+    to_x().wait_send()
+    diagonal(1).wait_send()
+    diagonal(2).wait_send()
+    for a, zs, zr, cs, cr in ((xl, *own_sems), (1 - xl, *far_sems)):
+        ring_last(a, zs, zr, 0).wait_send()
+        ring_last(a, zs, zr, 1).wait_send()
+
+        for s in range(1 if zs is zo_s else 3, 7):
+            ring(s, a, zs, zr).wait_send()
+        for s in range(STEPS):
+            to_core(s, a, cs, cr).wait_send()
+
+    ag_x_hidden(xh).wait_send()
+    for q in range(len(GROUPS)):
+        for j in (1, 2, 3):
+            y_send(q, j).wait_send()
+        x_send(q).wait_send()
+        ag_x(q).wait_send()
     assemble(0)
+    for p in range(len(PARTS)):
+        for up in (True, False):
+            ag_own(p, up).wait_send()
+            ag_pass(p, up).wait_send()
     assemble(1)
     total = ig_fin[...]
     for s in range(1, STEPS):
@@ -429,27 +457,6 @@
         outs.append(pltpu.make_async_copy(src, dst, out_sem.at[1 + i]))
         outs[-1].start()
 
-    to_x().wait_send()
-    diagonal(1).wait_send()
-    diagonal(2).wait_send()
-    for a, zs, zr, cs, cr in ((xl, *own_sems), (1 - xl, *far_sems)):
-        ring_last(a, zs, zr, 0).wait_send()
-        ring_last(a, zs, zr, 1).wait_send()
-
-        for s in range(1 if zs is zo_s else 3, 7):
-            ring(s, a, zs, zr).wait_send()
-        for s in range(STEPS):
-            to_core(s, a, cs, cr).wait_send()
-
-    for q in range(len(GROUPS)):
-        for j in (1, 2, 3):
-            y_send(q, j).wait_send()
-        x_send(q).wait_send()
-        ag_x(q).wait_send()
-    for p in range(len(PARTS)):
-        for up in (True, False):
-            ag_own(p, up).wait_send()
-            ag_pass(p, up).wait_send()
     for k in range(GU):
         for j in (1, 2, 3):
             piece(k, j).wait_send()
@@ -525,7 +532,7 @@
             dma, dma,
             dma((5, 3)), dma((5, 3)),
             dma((5,)), dma((5,)),
-            dma((5,)), dma((5,)),
+            dma((6,)), dma((6,)),
             dma((10, 2)), dma((10, 2)),
             dma((10, 2)), dma((10, 2)),
             dma((GU, 4)), dma((GU, 4)),

time: 108 us -> 107 us (level)
  no operation moved by 1% of the time
where the time goes in v4:
time: 107 us
  Pallas kernels  106 us (99%)
    pallas_call x1, Pallas kernels, on_device(): pl.pallas_call(kernel, out_shape=shapes, in_specs=[anyspace] * 5, out_spe...  103 us
    pallas_call x1, Pallas kernels, on_device(): pl.pallas_call(hand_on, out_shape=shapes, in_specs=[anyspace] * 4, out_sp...  2.7 us

profile of v4, /device:TPU:1, one launch (start us, length us, event | category | flops | bytes accessed | tf_op | source)
XLA Modules:
  0.0 106.5 jit_solution(15919884618612403730)
XLA Ops:
  0.6 103.2 %ffn_backward.1 = (bf16[32,896]{1,0:T(8,128)(2,1)}, bf16[224,1920]{1,0:T(8,128)(2,1)}, bf16[224,1920]{1,0:T(8,128)(2,1)}, bf16[480,896]{1,0:T(8,128)(2,1)}) custom-call(bf16[32,896]{1,0:T(8,128)(2,1)} %x_hbm.1, bf16[32,896]{1,0:T(8,128)(2,1)} %dy_hbm.1, bf16[896,1920]{1,0:T(8,128)(2,1)} %wg_hbm.1, bf16[896,1920]{1,0:T(8,128)(2,1)} %wu_hbm.1, ...), custom_call_target="tpu_custom_call" | custom-call | flops 8000000000 | bytes 12000000 | tf_op jit(solution)/shard_map/ffn_backward/pallas_call | solution.py:495
  103.8 2.7 %hand_on.1 = (bf16[32,896]{1,0:T(8,128)(2,1)}, bf16[224,1920]{1,0:T(8,128)(2,1)}, bf16[224,1920]{1,0:T(8,128)(2,1)}, bf16[480,896]{1,0:T(8,128)(2,1)}) custom-call(bf16[32,896]{1,0:T(8,128)(2,1)} %get-tuple-element.8.a0, bf16[224,1920]{1,0:T(8,128)(2,1)} %get-tuple-element.9.a1, bf16[224,1920]{1,0:T(8,128)(2,1)} %get-tuple-element.10.a2, ...), custom_call_target="tpu_custom_call" | custom-call | tf_op jit(solution)/shard_map/hand_on/pallas_call | solution.py:550

commit v5 on v4

--- a/solution.py
+++ b/solution.py
@@ -134,11 +134,11 @@
         return remote(block(0, xl, c), block(s, xl, c), zf_s.at[s], zf_r.at[s], dev)
 
     to_x().start()
+    to_core(0, xl, co_s, co_r).start()
     ring(1, xl, zo_s, zo_r).start()
     ring(2, xl, zo_s, zo_r).start()
     diagonal(1).start()
     diagonal(2).start()
-    to_core(0, xl, co_s, co_r).start()
 
     select(0)
     select(1)

time: 107 us -> 107 us (level)
  no operation moved by 1% of the time
where the time goes in v5:
time: 107 us
  Pallas kernels  106 us (99%)
    pallas_call x1, Pallas kernels, on_device(): pl.pallas_call(kernel, out_shape=shapes, in_specs=[anyspace] * 5, out_spe...  103 us
    pallas_call x1, Pallas kernels, on_device(): pl.pallas_call(hand_on, out_shape=shapes, in_specs=[anyspace] * 4, out_sp...  2.7 us

profile of v5, /device:TPU:1, one launch (start us, length us, event | category | flops | bytes accessed | tf_op | source)
XLA Modules:
  0.0 106.5 jit_solution(4690539640271206227)
XLA Ops:
  0.6 103.2 %ffn_backward.1 = (bf16[32,896]{1,0:T(8,128)(2,1)}, bf16[224,1920]{1,0:T(8,128)(2,1)}, bf16[224,1920]{1,0:T(8,128)(2,1)}, bf16[480,896]{1,0:T(8,128)(2,1)}) custom-call(bf16[32,896]{1,0:T(8,128)(2,1)} %x_hbm.1, bf16[32,896]{1,0:T(8,128)(2,1)} %dy_hbm.1, bf16[896,1920]{1,0:T(8,128)(2,1)} %wg_hbm.1, bf16[896,1920]{1,0:T(8,128)(2,1)} %wu_hbm.1, ...), custom_call_target="tpu_custom_call" | custom-call | flops 8000000000 | bytes 12000000 | tf_op jit(solution)/shard_map/ffn_backward/pallas_call | solution.py:495
  103.8 2.7 %hand_on.1 = (bf16[32,896]{1,0:T(8,128)(2,1)}, bf16[224,1920]{1,0:T(8,128)(2,1)}, bf16[224,1920]{1,0:T(8,128)(2,1)}, bf16[480,896]{1,0:T(8,128)(2,1)}) custom-call(bf16[32,896]{1,0:T(8,128)(2,1)} %get-tuple-element.8.a0, bf16[224,1920]{1,0:T(8,128)(2,1)} %get-tuple-element.9.a1, bf16[224,1920]{1,0:T(8,128)(2,1)} %get-tuple-element.10.a2, ...), custom_call_target="tpu_custom_call" | custom-call | tf_op jit(solution)/shard_map/hand_on/pallas_call | solution.py:550
